TPU v7x, 128 devices: a whole 4x4x4 slice. The times are simulated.
128 devices in a mesh: row: 16 (over x, y), col: 8 (over z, core).
Axes of the slice: x: 4, y: 4, z: 4, core: 2. Of those that a mesh axis runs over, the one named last changes fastest.
Arguments:
- panel: bfloat16 [49152, 256], P('row', 'col'), as said below
- trailing: bfloat16 [49152, 16384], P('row', 'col'), may hold values from -6 to 6
- tile_list: int32 [352], P('row'), may hold values from 0 to 23, as said below
Outputs:
- triangle: float32 [256, 256], replicated
- top_rows: float32 [16384, 256], P('col')
- updated: bfloat16 [45056, 16384], P('row', 'col')
Inputs may be any that keep to these rules, and one draw needn't show every extreme that they name: `tile_list`: each aligned block of 22 entries (the entries of one index of row) lists distinct tile numbers of that group's 24 tiles in increasing order and always includes tile 24 - 1. `panel`: the active rows of every row group, and all active rows together, have full column rank with a condition number under 100.
All inputs are finite; a program needn't handle non-finite values.
Results may differ from a plain program's by a relative error of at most 0.0065.
Values may be sent and summed in bfloat16 or wider, within the bound.
A program may use at most 128 MiB of HBM per device.

v0:
```python
import jax
import jax.numpy as jnp
from jax import lax
from jax.sharding import PartitionSpec as P

TILE = 128


def sent_to_all(array, axis):
    copies = jnp.broadcast_to(array, (lax.axis_size(axis), *array.shape))
    return lax.all_to_all(copies, axis, split_axis=0, concat_axis=0, tiled=True)


def laid_out(pieces, dim):
    pieces = jnp.moveaxis(pieces, 0, dim)
    shape = pieces.shape
    return pieces.reshape(*shape[:dim], shape[dim] * shape[dim + 1], *shape[dim + 2 :])


def gather_directly(array, axis, dim):
    pieces = sent_to_all(array, axis)
    return laid_out(pieces, dim)


def taken_together(array, axis):
    everything = sent_to_all(array, axis)
    return jnp.sum(everything.astype(jnp.float32), axis=0)


def pick_tiles(whole, tile_list):
    tiled = whole.reshape(-1, TILE, whole.shape[1])
    return jnp.take(tiled, tile_list, axis=0).reshape(-1, whole.shape[1])


def local(panel, trailing, tile_list):
    panel_full = gather_directly(panel, "col", 1)
    act_panel = pick_tiles(panel_full, tile_list)
    act_trail = pick_tiles(trailing, tile_list)
    local_gram = lax.dot_general(
        act_panel, act_panel, (((0,), (0,)), ((), ())), preferred_element_type=jnp.float32
    )
    gram_matrix = taken_together(local_gram.astype(jnp.bfloat16), "row").astype(jnp.float32)
    lower_factor = jnp.linalg.cholesky(gram_matrix)
    triangle = lower_factor.T
    local_cross = lax.dot_general(
        act_trail, act_panel, (((0,), (0,)), ((), ())), preferred_element_type=jnp.float32
    )
    cross_sum = lax.psum(local_cross, "row")
    top_rows = jax.scipy.linalg.solve_triangular(lower_factor, cross_sum.T, lower=True).T
    coeff = jax.scipy.linalg.solve_triangular(
        lower_factor, top_rows.T, lower=True, trans=1
    ).T.astype(jnp.bfloat16)
    product = lax.dot_general(
        act_panel, coeff, (((1,), (1,)), ((), ())), preferred_element_type=jnp.float32
    )
    updated = (act_trail.astype(jnp.float32) - product).astype(jnp.bfloat16)
    return (triangle, top_rows, updated)


def solution(mesh):
    return jax.shard_map(
        local,
        mesh=mesh,
        in_specs=(P("row", "col"), P("row", "col"), P("row")),
        out_specs=(P(), P("col", None), P("row", "col")),
        check_vma=False,
    )
```

profile of v0, /device:TPU:1, one launch (start us, length us, event | category | flops | bytes accessed | tf_op | source)
XLA Modules:
  0.0 184.8 jit_solution(9979115760256562924)
XLA Ops:
  7.2 0.0 copy-start.2
  7.2 2.3 %broadcast_in_dim.43 = bf16[8,3072,32]{1,2,0:T(8,128)(2,1)} broadcast(bf16[3072,32]{0,1:T(8,128)(2,1)} %param.3), dimensions={1,2} | broadcast | bytes 1769472 | tf_op jit(solution)/shard_map/broadcast_in_dim | solution.py:10
  9.4 6.8 %all-to-all-start = ((bf16[8,3072,32]{1,2,0:T(8,128)(2,1)}), bf16[8,3072,32]{1,2,0:T(8,128)(2,1)S(1)}, u32[]{:S(2)}, u32[]{:S(2)}) async-start(bf16[8,3072,32]{1,2,0:T(8,128)(2,1)} %broadcast_in_dim.43), calls=%async_computation | async-start | bytes 3145728 | tf_op jit(solution)/shard_map/all_to_all | solution.py:11
  16.2 0.0 copy-done.2
  16.3 0.1 broadcast_bitcast_fusion
  16.4 20.6 %all-to-all-done = bf16[8,3072,32]{1,2,0:T(8,128)(2,1)S(1)} async-done(((bf16[8,3072,32]{1,2,0:T(8,128)(2,1)}), bf16[8,3072,32]{1,2,0:T(8,128)(2,1)S(1)}, u32[]{:S(2)}, u32[]{:S(2)}) %all-to-all-start) | async-done | bytes 1572896 | tf_op jit(solution)/shard_map/all_to_all | solution.py:11
  37.0 0.3 copy.25
  37.3 1.1 copy.17
  38.4 0.6 gather_fusion
  39.1 0.9 fusion.7
  40.0 1.5 broadcast_in_dim.46
  41.5 6.8 %all-to-all-start.1 = ((bf16[16,256,256]{2,1,0:T(8,128)(2,1)}), bf16[16,256,256]{2,1,0:T(8,128)(2,1)S(1)}, u32[]{:S(2)}, u32[]{:S(2)}) async-start(bf16[16,256,256]{2,1,0:T(8,128)(2,1)} %broadcast_in_dim.46), calls=%async_computation.1 | async-start | bytes 4194304 | tf_op jit(solution)/shard_map/all_to_all | solution.py:11
  48.2 0.0 all-reduce.3.cloned.1.call-start
  48.3 10.5 %gather_fusion.1 = bf16[22,128,2048]{2,1,0:T(8,128)(2,1)} fusion(bf16[24,128,2048]{2,1,0:T(8,128)(2,1)} %bitcast.64, s32[1024]{0:T(1024)S(1)} %pad_clamp_fusion), kind=kCustom, calls=%fused_computation.1 | custom fusion | bytes 23068760 | tf_op jit(solution)/shard_map/jit(_take)/gather | solution.py:32
  58.8 8.8 %fusion.4 = f32[256,2048]{1,0:T(8,128)} fusion(bf16[22,128,2048]{2,1,0:T(8,128)(2,1)} %gather_fusion.1, pred[22]{0:T(512)(128)(4,1)S(1)} %compare_and_fusion, bf16[22,128,256]{2,1,0:T(8,128)(2,1)S(1)} %gather_fusion), kind=kOutput, calls=%fused_computation.11 | convolution fusion | flops 2959278080 | bytes 15073302 | tf_op jit(solution)/shard_map/dot_general | solution.py:45
  67.6 0.0 all-reduce.3.cloned.1.call-update
  67.7 2.3 %bitcast_select_fusion.1 = bf16[2816,256]{1,0:T(8,128)(2,1)} fusion(bf16[22,128,256]{2,1,0:T(8,128)(2,1)S(1)} %gather_fusion, pred[2816]{0:T(1024)(128)(4,1)S(1)} %broadcast_bitcast_fusion), kind=kLoop, calls=%fused_computation.16 | loop fusion | flops 720896 | bytes 2886400 | tf_op jit(solution)/shard_map/jit(_take)/select_n | solution.py:32
  70.0 4.7 %all-to-all-done.1 = bf16[16,256,256]{2,1,0:T(8,128)(2,1)S(1)} async-done(((bf16[16,256,256]{2,1,0:T(8,128)(2,1)}), bf16[16,256,256]{2,1,0:T(8,128)(2,1)S(1)}, u32[]{:S(2)}, u32[]{:S(2)}) %all-to-all-start.1) | async-done | bytes 2097184 | tf_op jit(solution)/shard_map/all_to_all | solution.py:11
  74.7 0.3 convert_reduce_fusion
  75.0 0.1 copy.19
  75.2 11.7 %cholesky.50 = f32[128,128]{1,0:T(8,128)S(1)} custom-call(f32[128,128]{1,0:T(8,128)S(1)} %cholesky.118), custom_call_target="Cholesky" | custom-call | tf_op jit(solution)/shard_map/jit(cholesky)/cholesky | solution.py:43
  86.9 9.8 %custom-call.18 = f32[1,128,128]{1,2,0:T(8,128)S(1)} custom-call(f32[1,128,128]{2,1,0:T(8,128)S(1)} %get-tuple-element.35), custom_call_target="InvertDiagBlocksLowerTriangular" | custom-call | tf_op jit(solution)/shard_map/jit(cholesky)/cholesky | solution.py:43
  96.8 0.2 constant_dynamic-update-slice_fusion.1
  97.0 0.3 convolution_subtract_fusion.2
  97.3 11.7 %cholesky.105 = f32[128,128]{1,0:T(8,128)S(1)} custom-call(f32[128,128]{1,0:T(8,128)S(1)} %convolution_subtract_fusion.2), custom_call_target="Cholesky" | custom-call | tf_op jit(solution)/shard_map/jit(cholesky)/cholesky | solution.py:43
  109.0 0.6 compare_reduce_fusion
  111.0 0.8 copy.21
  111.9 0.1 triangular_solve.53
  111.9 5.2 %while.1 = (s32[]{:T(128)}, f32[256,256]{1,0:T(8,128)S(1)}, s32[2,2]{1,0:T(2,128)S(1)}, f32[2,128,128]{2,1,0:T(8,128)}, s32[]{:T(128)}) while((s32[]{:T(128)}, f32[256,256]{1,0:T(8,128)S(1)}, s32[2,2]{1,0:T(2,128)S(1)}, f32[2,128,128]{2,1,0:T(8,128)}, s32[]{:T(128)}) %tuple.32), condition=%wide.while_cond, body=%wide.while_body.sunk | while | flops 2 | bytes 132205 | solution.py:49
  111.9 0.6 fusion.37
  112.5 2.0 %bitcast_dynamic-update-slice_fusion.2 = f32[2,128,128]{2,1,0:T(8,128)} fusion(f32[2,128,128]{2,1,0:T(8,128)} %get-tuple-element.79, s32[]{:T(128)S(6)} %copy.32, f32[256,256]{1,0:T(8,128)S(1)} %get-tuple-element.82, s32[]{:T(128)} %bitcast.62, s32[]{:T(128)} %bitcast.63), kind=kLoop, calls=%fused_computation.2.clone.1 | loop fusion | bytes 132100 | tf_op jit(solution)/shard_map/jit(_solve_triangular)/triangular_solve
  114.5 0.6 fusion.37
  115.1 2.0 %bitcast_dynamic-update-slice_fusion.2 = f32[2,128,128]{2,1,0:T(8,128)} fusion(f32[2,128,128]{2,1,0:T(8,128)} %get-tuple-element.79, s32[]{:T(128)S(6)} %copy.32, f32[256,256]{1,0:T(8,128)S(1)} %get-tuple-element.82, s32[]{:T(128)} %bitcast.62, s32[]{:T(128)} %bitcast.63), kind=kLoop, calls=%fused_computation.2.clone.1 | loop fusion | bytes 132100 | tf_op jit(solution)/shard_map/jit(_solve_triangular)/triangular_solve
  117.1 20.5 %custom-call.19 = f32[2,128,128]{1,2,0:T(8,128)S(1)} custom-call(f32[2,128,128]{2,1,0:T(8,128)} %get-tuple-element.10), custom_call_target="InvertDiagBlocksLowerTriangular" | custom-call | tf_op jit(solution)/shard_map/jit(_solve_triangular)/triangular_solve | solution.py:49
  137.6 19.7 %all-reduce.3.cloned.1.call-done = f32[256,2048]{1,0:T(8,128)} async-done(((f32[256,2048]{1,0:T(8,128)}), f32[256,2048]{1,0:T(8,128)}) %all-reduce.3.cloned.1.call-update) | async-done | bytes 2097168 | tf_op jit(solution)/shard_map/psum | solution.py:48
  157.3 0.0 copy-start
  157.3 2.4 %fusion.8 = f32[128,2048]{1,0:T(8,128)S(1)} fusion(f32[256,2048]{1,0:T(8,128)} %all-reduce.3.cloned.1.call-done, f32[2,128,128]{1,2,0:T(8,128)S(1)} %custom-call.19), kind=kOutput, calls=%fused_computation.21 | convolution fusion | flops 402653184 | bytes 2162688 | tf_op jit(solution)/shard_map/jit(_solve_triangular)/triangular_solve | solution.py:49
  159.7 0.0 copy-done
  159.8 1.0 convolution_subtract_fusion.1
  160.8 1.1 fusion.20
  161.8 1.8 fusion.27
  163.6 0.1 maximum_bitcast_fusion
  163.8 1.1 convolution_subtract_fusion
  164.9 1.8 convolution_convert_fusion
  166.7 0.0 copy-start.1
  166.7 1.8 copy.22
  168.5 0.0 copy-done.1
  168.5 9.5 %subtract_convert_fusion = bf16[2816,2048]{1,0:T(8,128)(2,1)} fusion(bf16[22,128,2048]{2,1,0:T(8,128)(2,1)} %gather_fusion.1, pred[2816]{0:T(1024)(128)(4,1)S(1)} %broadcast_bitcast_fusion, bf16[2816,256]{1,0:T(8,128)(2,1)S(1)} %copy-done.1, bf16[128,2048]{1,0:T(8,128)(2,1)} %get-tuple-element.38, bf16[128,2048]{1,0:T(8,128)(2,1)} %convolution_convert_fusion), kind=kOutput, calls=%fused_computation.4 | convolution fusion | flops 2977955840 | bytes 25561856 | tf_op jit(solution)/shard_map/dot_general | solution.py:53
  (13 shorter events, 0.2 us)
Async XLA Ops:
  7.2 9.1 %copy-start.2 = (s32[22]{0:T(128)S(1)}, s32[22]{0:T(128)}, u32[]{:S(2)}) copy-start(s32[22]{0:T(128)} %param.5) | copy-start | bytes 268
  9.4 27.5 %all-to-all-start = ((bf16[8,3072,32]{1,2,0:T(8,128)(2,1)}), bf16[8,3072,32]{1,2,0:T(8,128)(2,1)S(1)}, u32[]{:S(2)}, u32[]{:S(2)}) async-start(bf16[8,3072,32]{1,2,0:T(8,128)(2,1)} %broadcast_in_dim.43), calls=%async_computation | async-start | bytes 3145728 | tf_op jit(solution)/shard_map/all_to_all | solution.py:11
  41.5 33.2 %all-to-all-start.1 = ((bf16[16,256,256]{2,1,0:T(8,128)(2,1)}), bf16[16,256,256]{2,1,0:T(8,128)(2,1)S(1)}, u32[]{:S(2)}, u32[]{:S(2)}) async-start(bf16[16,256,256]{2,1,0:T(8,128)(2,1)} %broadcast_in_dim.46), calls=%async_computation.1 | async-start | bytes 4194304 | tf_op jit(solution)/shard_map/all_to_all | solution.py:11
  48.2 109.1 %all-reduce.3.cloned.1.call-start = ((), (), s32[]{:S(2)}) async-start(), calls=%async_computation.2 | async-start | bytes 4194304 | tf_op jit(solution)/shard_map/psum | solution.py:48
  157.3 2.4 %copy-start = (f32[256,2048]{1,0:T(8,128)S(1)}, f32[256,2048]{1,0:T(8,128)}, u32[]{:S(2)}) copy-start(f32[256,2048]{1,0:T(8,128)} %all-reduce.3.cloned.1.call-done) | copy-start | bytes 6291460
  166.7 1.8 copy-start.1
Sparse Core Ops, SparseCore 0:
  67.8 89.5 all-reduce.2
where the time goes:
time: 186 us; the launch traced here: 185 us
  other arithmetic  57.3 us (31%)
  waiting for transfers between devices  45.1 us (24%)
  matrix products  28.8 us (15%)
  local copies, waits for them, and re-layouts  24.5 us (13%)
  between operations  15.5 us (8%)
  starting transfers between devices  13.6 us (7%)
    another operation x6, other arithmetic, local(): lower_factor = jnp.linalg.cholesky(gram_matrix)  34 us
    all_to_all x2, waiting for transfers between devices, sent_to_all(): return lax.all_to_all(copies, axis, split_axis=0, concat_axis=0, tiled=True)  25.3 us
    another operation x3, other arithmetic, local(): jax.scipy.linalg.solve_triangular(lower_factor, cross_sum.T, lower=True)  20.5 us
    psum x1, waiting for transfers between devices, local(): cross_sum = lax.psum(local_cross, 'row')  19.7 us
    all_to_all x2, starting transfers between devices, sent_to_all(): return lax.all_to_all(copies, axis, split_axis=0, concat_axis=0, tiled=True)  13.6 us
    gather x2, local copies, waits for them, and re-layouts, pick_tiles(): return jnp.take(tiled, tile_list, axis=0).reshape(-1, whole.shape[1])  11.1 us
    dot_general x1, matrix products, local(): lax.dot_general(act_panel, coeff, (((1,), (1,)), ((), ())), preferred_ele...  9.5 us
    dot_general x1, matrix products, local(): lax.dot_general(act_trail, act_panel, (((0,), (0,)), ((), ())), preferred...  8.84 us
  transfers between devices with their start and end apart: 3, of which 3 were waited for; matrix products, arithmetic and copies ran while one was open for 45% of the time, Pallas kernels for 0%

commit v1 on v0

v1 whole, which is shorter than its diff:
```python
import functools

import jax
import jax.numpy as jnp
from jax import lax
from jax.experimental import pallas as pl
from jax.experimental.pallas import tpu as pltpu
from jax.sharding import PartitionSpec as P

TILE = 128
MESH = pl.DeviceIdType.MESH
F32 = jnp.float32
BF16 = jnp.bfloat16
HIGH = lax.Precision.HIGHEST


def dot(a, b, dims, precision=None):
    return lax.dot_general(a, b, (dims, ((), ())), precision=precision, preferred_element_type=F32)


def factor(a_ref, u_ref, m_ref, n, block):
    for k in range(n // block):
        lo = k * block
        slab = a_ref[lo : lo + block, :]
        rows = lax.broadcasted_iota(jnp.int32, (block, 1), 0)
        for j in range(block):
            scale = lax.rsqrt(slab[j : j + 1, lo + j : lo + j + 1])
            row = slab[j : j + 1, :] * scale
            col = slab[:, lo + j : lo + j + 1] * scale
            col = jnp.where(rows > j, col, 0.0)
            slab = jnp.where(rows == j, row, slab - col * row)
        u = slab[:, :n]
        cols = lax.broadcasted_iota(jnp.int32, (block, n), 1)
        keep = cols >= lax.broadcasted_iota(jnp.int32, (block, n), 0) + lo
        u_ref[lo : lo + block, :] = jnp.where(keep, u, 0.0)
        m_ref[lo : lo + block, :] = slab[:, n:]
        if lo + block < n:
            a_ref[lo + block :, :] -= dot(slab[:, lo + block : n], slab, ((0,), (0,)), HIGH)


def fetch_and_reduce(
    tl_ref, pt_ref, t_hbm,
    t_out, pt_out, cr_out, u_out, m_out,
    wide, gx, gy, gc, aug, s1, l1, s2, l2, agb,
    t_sem, p_send, p_recv, g_send, g_recv, c_send, c_recv,
):
    width, active = pt_ref.shape[0], tl_ref.shape[0]
    n = 8 * width
    tiles = t_out.shape[0]
    spare = tiles - active
    r, c = lax.axis_index("row"), lax.axis_index("col")
    x, y, z, k = r // 4, lax.rem(r, 4), c // 2, lax.rem(c, 2)

    def along_x(d):
        return (lax.rem(x + d, 4) * 4 + y, c)

    def along_y(d):
        return (x * 4 + lax.rem(y + d, 4), c)

    def along_z(d):
        return (r, lax.rem(z + d, 4) * 2 + k)

    sibling = (r, z * 2 + 1 - k)

    loads = []
    for i in range(6):
        copy = pltpu.make_async_copy(t_hbm.at[pl.ds(4 * i, 4)], t_out.at[pl.ds(4 * i, 4)], t_sem.at[i])
        copy.start()
        loads.append(copy)

    barrier = pltpu.get_barrier_semaphore()
    partners = [f(d) for f in (along_x, along_y, along_z) for d in (1, 2, 3)] + [sibling]
    for partner in partners:
        pl.semaphore_signal(barrier, inc=1, device_id=partner, device_id_type=MESH)

    for j in range(active):
        pick = pt_ref[:, (j + spare) * TILE : (j + spare + 1) * TILE]
        for i in reversed(range(spare)):
            pick = jnp.where(tl_ref[j] == j + i, pt_ref[:, (j + i) * TILE : (j + i + 1) * TILE], pick)
        pt_out[c, :, j * TILE : (j + 1) * TILE] = pick
    pl.semaphore_wait(barrier, len(partners))

    def send(src, dst, send_sem, recv_sem, to):
        copy = pltpu.make_async_remote_copy(
            src_ref=src, dst_ref=dst, send_sem=send_sem, recv_sem=recv_sem, device_id=to, device_id_type=MESH
        )
        copy.start()
        return copy

    def gather_col(ref, sends, recvs, base):
        mine = ref.at[c]
        out = [send(mine, mine, sends.at[base], recvs.at[base], sibling)]
        direct = {}
        for i, d in enumerate((1, 3, 2)):
            direct[d] = send(mine, mine, sends.at[base + 1 + i], recvs.at[base + 1 + i], along_z(d))
        return out, direct

    def relay_col(ref, sends, recvs, base, started):
        out, direct = started
        for i, d in enumerate((1, 3, 2)):
            direct[d].wait_recv()
            owner = ref.at[lax.rem(z + 4 - d, 4) * 2 + k]
            out.append(send(owner, owner, sends.at[base + 4 + i], recvs.at[base + 4 + i], sibling))
        for copy in out:
            copy.wait()
        for d in (1, 3, 2):
            direct[d].wait_send()

    started = gather_col(pt_out, p_send, p_recv, 0)
    relay_col(pt_out, p_send, p_recv, 0, started)

    pt_all = pt_out[...].reshape(n, active * TILE)
    gx[x] = dot(pt_out[c], pt_all, ((1,), (1,)))
    for j in range(tiles):
        spread = jnp.zeros((8, width, TILE), BF16)
        for i in range(max(j - spare, 0), min(j, active - 1) + 1):
            spread = jnp.where(tl_ref[i] == j, pt_out[:, :, i * TILE : (i + 1) * TILE], spread)
        wide[:, j * TILE : (j + 1) * TILE] = spread.reshape(n, TILE)
    g1 = [send(gx.at[x], gx.at[x], g_send.at[d - 1], g_recv.at[d - 1], along_x(d)) for d in (1, 2, 3)]

    for copy in loads:
        copy.wait()

    def first(q):
        return (along_x, along_y, x, y) if q % 2 == 0 else (along_y, along_x, y, x)

    def cross(q):
        for half in range(2):
            cols = slice(q * 512 + half * 256, q * 512 + half * 256 + 256)
            part = dot(wide[...], t_out[:, :, cols].reshape(tiles * TILE, 256), ((1,), (0,)))
            s1[q, 2 * half] = part[:, :128].astype(BF16)
            s1[q, 2 * half + 1] = part[:, 128:].astype(BF16)
        a, _, ma, _ = first(q)
        sent = []
        for d in (1, 2, 3):
            sem = 12 * q + d - 1
            sent.append(send(s1.at[q, lax.rem(ma + d, 4)], l1.at[q, d - 1], c_send.at[sem], c_recv.at[sem], a(d)))
        return sent

    stage1 = [cross(0)]
    for copy in g1:
        copy.wait()
    gy[y] = gx[0] + gx[1] + gx[2] + gx[3]
    g2 = [send(gy.at[y], gy.at[y], g_send.at[2 + d], g_recv.at[2 + d], along_y(d)) for d in (1, 2, 3)]
    stage1.append(cross(1))
    for copy in g2:
        copy.wait()
    gc[c] = gy[0] + gy[1] + gy[2] + gy[3]
    g3 = gather_col(gc, g_send, g_recv, 6)
    stage1.append(cross(2))
    stage1.append(cross(3))

    stage2 = []
    for q in range(4):
        _, b, ma, mb = first(q)
        for copy in stage1[q]:
            copy.wait()
        total = s1[q, ma].astype(F32)
        for d in range(3):
            total = total + l1[q, d].astype(F32)
        s2[q] = total.astype(BF16).reshape(4, n // 4, 128)
        sent = []
        for d in (1, 2, 3):
            sem = 12 * q + 2 + d
            sent.append(send(s2.at[q, lax.rem(mb + d, 4)], l2.at[q, d - 1], c_send.at[sem], c_recv.at[sem], b(d)))
        stage2.append(sent)
    stage3 = []
    for q in range(4):
        _, b, ma, mb = first(q)
        for copy in stage2[q]:
            copy.wait()
        total = s2[q, mb].astype(F32)
        for d in range(3):
            total = total + l2[q, d].astype(F32)
        agb[q, mb] = total.astype(BF16)
        sent = []
        for d in (1, 2, 3):
            sem = 12 * q + 5 + d
            sent.append(send(agb.at[q, mb], agb.at[q, mb], c_send.at[sem], c_recv.at[sem], b(d)))
        stage3.append(sent)
    relay_col(gc, g_send, g_recv, 6, g3)
    stage4 = []
    for q in range(4):
        a, _, ma, _ = first(q)
        for copy in stage3[q]:
            copy.wait()
        cr_out[q, ma] = agb[q].reshape(n, 128)
        sent = []
        for d in (1, 2, 3):
            sem = 12 * q + 8 + d
            sent.append(send(cr_out.at[q, ma], cr_out.at[q, ma], c_send.at[sem], c_recv.at[sem], a(d)))
        stage4.append(sent)

    aug[:, :n] = gc[...].reshape(n, n)
    eye = lax.broadcasted_iota(jnp.int32, (n, n), 0) == lax.broadcasted_iota(jnp.int32, (n, n), 1)
    aug[:, n:] = jnp.where(eye, 1.0, 0.0)
    factor(aug, u_out, m_out, n, 32)
    for sent in stage4:
        for copy in sent:
            copy.wait()


def finish(tl_ref, t_ref, pt_ref, cr_ref, u_ref, m_ref, tri_ref, top_hbm, up_hbm, coeff, tops, outs, top_sem, out_sem):
    n = m_ref.shape[0]
    active = tl_ref.shape[0]
    tri_ref[...] = u_ref[...]
    m = m_ref[...]
    mh = m.astype(BF16)
    ml = (m - mh.astype(F32)).astype(BF16)
    copies = []
    for q in range(4):
        part = jnp.concatenate([cr_ref[q, a] for a in range(4)], axis=1)
        top = dot(mh, part, ((1,), (0,))) + dot(ml, part, ((1,), (0,)))
        tops[q] = top.T
        copy = pltpu.make_async_copy(tops.at[q], top_hbm.at[pl.ds(q * 512, 512)], top_sem.at[q])
        copy.start()
        copies.append(copy)
        tb = top.astype(BF16)
        coeff[:, q * 512 : (q + 1) * 512] = (dot(mh, tb, ((0,), (0,))) + dot(ml, tb, ((0,), (0,)))).astype(BF16)
    pending = [None] * 3
    for i in range(active // 2):
        slot = i % 3
        if pending[slot] is not None:
            pending[slot].wait()
        cols = pt_ref[:, :, i * 256 : (i + 1) * 256].reshape(n, 256)
        product = dot(cols, coeff[...], ((0,), (0,)))
        outs[slot, :128] = (t_ref[tl_ref[2 * i]].astype(F32) - product[:128]).astype(BF16)
        outs[slot, 128:] = (t_ref[tl_ref[2 * i + 1]].astype(F32) - product[128:]).astype(BF16)
        copy = pltpu.make_async_copy(outs.at[slot], up_hbm.at[pl.ds(i * 256, 256)], out_sem.at[slot])
        copy.start()
        pending[slot] = copy
    for copy in pending + copies:
        copy.wait()


def local(panel, trailing, tile_list):
    rows, width = panel.shape
    cols = trailing.shape[1]
    active = tile_list.shape[0]
    tiles = rows // TILE
    n = 8 * width
    vmem = pl.BlockSpec(memory_space=pltpu.VMEM)
    smem = pl.BlockSpec(memory_space=pltpu.SMEM)
    anywhere = pl.BlockSpec(memory_space=pl.ANY)
    hbm = pl.BlockSpec(memory_space=pltpu.HBM)
    dma = pltpu.SemaphoreType.DMA
    t, pt, cr, u, m = pl.pallas_call(
        fetch_and_reduce,
        out_shape=(
            pltpu.VMEM((tiles, TILE, cols), BF16),
            pltpu.VMEM((8, width, active * TILE), BF16),
            pltpu.VMEM((4, 4, n, 128), BF16),
            pltpu.VMEM((n, n), F32),
            pltpu.VMEM((n, n), F32),
        ),
        in_specs=[smem, vmem, hbm],
        out_specs=[vmem] * 5,
        scratch_shapes=[
            pltpu.VMEM((n, rows), BF16),
            pltpu.VMEM((4, width, n), F32),
            pltpu.VMEM((4, width, n), F32),
            pltpu.VMEM((8, width, n), F32),
            pltpu.VMEM((n, 2 * n), F32),
            pltpu.VMEM((4, 4, n, 128), BF16),
            pltpu.VMEM((4, 3, n, 128), BF16),
            pltpu.VMEM((4, 4, n // 4, 128), BF16),
            pltpu.VMEM((4, 3, n // 4, 128), BF16),
            pltpu.VMEM((4, 4, n // 4, 128), BF16),
            dma((6,)),
            dma((7,)),
            dma((7,)),
            dma((13,)),
            dma((13,)),
            dma((48,)),
            dma((48,)),
        ],
        compiler_params=pltpu.CompilerParams(collective_id=0, has_side_effects=True, vmem_limit_bytes=24 * 2**20),
    )(tile_list, panel.T, trailing.reshape(tiles, TILE, cols))
    return pl.pallas_call(
        finish,
        out_shape=(
            jax.ShapeDtypeStruct((n, n), F32),
            jax.ShapeDtypeStruct((cols, n), F32),
            jax.ShapeDtypeStruct((active * TILE, cols), BF16),
        ),
        in_specs=[smem] + [vmem] * 5,
        out_specs=[vmem, anywhere, anywhere],
        scratch_shapes=[
            pltpu.VMEM((n, cols), BF16),
            pltpu.VMEM((4, cols // 4, n), F32),
            pltpu.VMEM((3, 2 * TILE, cols), BF16),
            dma((4,)),
            dma((3,)),
        ],
        compiler_params=pltpu.CompilerParams(vmem_limit_bytes=24 * 2**20),
    )(tile_list, t, pt, cr, u, m)


def solution(mesh):
    return jax.shard_map(
        local,
        mesh=mesh,
        in_specs=(P("row", "col"), P("row", "col"), P("row")),
        out_specs=(P(), P("col", None), P("row", "col")),
        check_vma=False,
    )
```

time: 186 us -> 87.7 us (0.47)
  the two profiles are of different devices: /device:TPU:1 before, /device:TPU:0 now
where the time goes in v1:
time: 87.7 us; the launch traced here: 87.5 us
  Pallas kernels  80.5 us (92%)
  local copies, waits for them, and re-layouts  6.15 us (7%)
    pallas_call x1, Pallas kernels, local(): pl.pallas_call(fetch_and_reduce, out_shape=(pltpu.VMEM((tiles, TILE, cols...  70.9 us
    pallas_call x1, Pallas kernels, local(): pl.pallas_call(finish, out_shape=(jax.ShapeDtypeStruct((n, n), F32), jax....  9.64 us
    unnamed x6, local copies, waits for them, and re-layouts  6.15 us

profile of v1, /device:TPU:0, one launch (start us, length us, event | category | flops | bytes accessed | tf_op | source)
XLA Modules:
  0.0 87.5 jit_solution(11463633639203694796)
XLA Ops:
  0.6 0.0 copy-start
  0.6 4.6 %copy-done = bf16[3072,2048]{1,0:T(8,128)(2,1)S(1)} copy-done((bf16[3072,2048]{1,0:T(8,128)(2,1)S(1)}, bf16[3072,2048]{1,0:T(8,128)(2,1)}, u32[]{:S(2)}) %copy-start) | copy-done | bytes 12582936
  5.2 0.0 copy-start.1
  5.2 0.9 %copy-done.1 = bf16[3072,32]{0,1:T(8,128)(2,1)S(1)} copy-done((bf16[3072,32]{0,1:T(8,128)(2,1)S(1)}, bf16[3072,32]{0,1:T(8,128)(2,1)}, u32[]{:S(2)}) %copy-start.1) | copy-done | bytes 196632
  6.1 0.0 copy-start.2
  6.1 0.7 copy-done.2
  6.8 70.9 %shard_map.58 = (bf16[24,128,2048]{2,1,0:T(8,128)(2,1)S(1)}, bf16[8,32,2816]{2,1,0:T(8,128)(2,1)S(1)}, bf16[4,4,256,128]{3,2,1,0:T(8,128)(2,1)S(1)}, f32[256,256]{1,0:T(8,128)S(1)}, f32[256,256]{1,0:T(8,128)S(1)}) custom-call(s32[22]{0:T(128)S(1)} %copy-done.2, bf16[32,3072]{1,0:T(8,128)(2,1)S(1)} %bitcast.3, bf16[24,128,2048]{2,1,0:T(8,128)(2,1)S(1)} %bitcast.2), custom_call_target="tpu_custom_call" | custom-call | tf_op jit(solution)/shard_map/pallas_call | solution.py:247
  77.7 9.6 %shard_map.59 = (f32[256,256]{1,0:T(8,128)}, f32[2048,256]{1,0:T(8,128)}, bf16[2816,2048]{1,0:T(8,128)(2,1)}) custom-call(s32[22]{0:T(128)S(1)} %copy-done.2, bf16[24,128,2048]{2,1,0:T(8,128)(2,1)S(1)} %get-tuple-element.8.t_ref, bf16[8,32,2816]{2,1,0:T(8,128)(2,1)S(1)} %get-tuple-element.9.pt_ref, bf16[4,4,256,128]{3,2,1,0:T(8,128)(2,1)S(1)} %get-tuple-element.10.cr_ref, ...), custom_call_target="tpu_custom_call" | custom-call | tf_op jit(solution)/shard_map/pallas_call | solution.py:279
Async XLA Ops:
  0.6 4.6 %copy-start = (bf16[3072,2048]{1,0:T(8,128)(2,1)S(1)}, bf16[3072,2048]{1,0:T(8,128)(2,1)}, u32[]{:S(2)}) copy-start(bf16[3072,2048]{1,0:T(8,128)(2,1)} %param.4) | copy-start | bytes 37748740
  5.2 0.9 %copy-start.1 = (bf16[3072,32]{0,1:T(8,128)(2,1)S(1)}, bf16[3072,32]{0,1:T(8,128)(2,1)}, u32[]{:S(2)}) copy-start(bf16[3072,32]{0,1:T(8,128)(2,1)} %param.3) | copy-start | bytes 589828
  6.1 0.7 copy-start.2

commit v2 on v0

v2 whole, which is shorter than its diff:
```python
import functools

import jax
import jax.numpy as jnp
from jax import lax
from jax.experimental import pallas as pl
from jax.experimental.pallas import tpu as pltpu
from jax.sharding import PartitionSpec as P

TILE = 128
MESH = pl.DeviceIdType.MESH
F32 = jnp.float32
BF16 = jnp.bfloat16
HIGH = lax.Precision.HIGHEST


def dot(a, b, dims, precision=None):
    return lax.dot_general(a, b, (dims, ((), ())), precision=precision, preferred_element_type=F32)


def spread_entries(d, p):
    a, low, inv = {}, {}, {}
    for i in range(p):
        for j in range(i + 1):
            a[i, j] = jnp.broadcast_to(d[j : j + 1, i : i + 1], (8, 128))
    for j in range(p):
        inv[j, j] = lax.rsqrt(a[j, j])
        for i in range(j, p):
            low[i, j] = a[i, j] * inv[j, j]
        for k in range(j + 1, p):
            for i in range(k, p):
                a[i, k] = a[i, k] - low[i, j] * low[k, j]
    for i in range(p):
        for j in range(i):
            total = sum(low[i, k] * inv[k, j] for k in range(j, i))
            inv[i, j] = -total * inv[i, i]
    return inv


def factor(a_ref, u_ref, m_ref, n, block, p=8):
    wide = 2 * n // 128
    rows = lax.broadcasted_iota(jnp.int32, (8, 128), 0)

    def across(column):
        return jnp.concatenate([column] * wide, axis=1)

    for lo in range(0, n, block):
        groups = [a_ref[lo + i : lo + i + p, :] for i in range(0, block, p)]
        done = []
        for g in range(block // p):
            at = lo + g * p
            inv = spread_entries(groups[g][:, at : at + p], p)
            u = None
            for j in range(p):
                column = jnp.zeros((8, 128), F32)
                for i in range(j, p):
                    column = jnp.where(rows == i, inv[i, j], column)
                term = across(column) * groups[g][j : j + 1, :]
                u = term if u is None else u + term
            done.append(u)
            for h in range(g + 1, block // p):
                left = [jnp.broadcast_to(groups[h][:, at + q : at + q + 1], (8, 128)) for q in range(p)]
                rest = groups[h]
                for j in range(p):
                    column = sum(left[q] * inv[j, q] for q in range(j + 1))
                    rest = rest - across(column) * u[j : j + 1, :]
                groups[h] = rest
            yield
        full = jnp.concatenate(done, axis=0)
        keep = lax.broadcasted_iota(jnp.int32, (block, n), 1) >= lax.broadcasted_iota(jnp.int32, (block, n), 0) + lo
        u_ref[lo : lo + block, :] = jnp.where(keep, full[:, :n], 0.0)
        m_ref[lo : lo + block, :] = full[:, n:]
        if lo + block < n:
            a_ref[lo + block :, :] -= dot(full[:, lo + block : n], full, ((0,), (0,)), HIGH)


def fetch_and_reduce(
    tl_ref, pt_ref, t_hbm,
    t_out, pt_out, cr_out, u_out, m_out,
    wide, gx, gy, gz, aug, s1, l1, s2,
    t_sem, p_send, p_recv, g_send, g_recv, c_send, c_recv,
):
    width, active = pt_ref.shape[0], tl_ref.shape[0]
    n = 8 * width
    pair = 2 * width
    tiles = t_out.shape[0]
    spare = tiles - active
    part = t_out.shape[2] // 4
    r, c = lax.axis_index("row"), lax.axis_index("col")
    x, y, z, k = r // 4, lax.rem(r, 4), c // 2, lax.rem(c, 2)

    def along_x(d):
        return (lax.rem(x + d, 4) * 4 + y, c)

    def along_y(d):
        return (x * 4 + lax.rem(y + d, 4), c)

    def along_z(d):
        return (r, lax.rem(z + d, 4) * 2 + k)

    sibling = (r, z * 2 + 1 - k)

    barrier = pltpu.get_barrier_semaphore()
    partners = [f(d) for f in (along_x, along_y, along_z) for d in (1, 2, 3)] + [sibling]
    for partner in partners:
        pl.semaphore_signal(barrier, inc=1, device_id=partner, device_id_type=MESH)

    loads = []
    for i in range(6):
        copy = pltpu.make_async_copy(t_hbm.at[pl.ds(4 * i, 4)], t_out.at[pl.ds(4 * i, 4)], t_sem.at[i])
        copy.start()
        loads.append(copy)

    for j in range(active):
        pick = pt_ref[:, (j + spare) * TILE : (j + spare + 1) * TILE]
        for i in reversed(range(spare)):
            pick = jnp.where(tl_ref[j] == j + i, pt_ref[:, (j + i) * TILE : (j + i + 1) * TILE], pick)
        pt_out[z, k, :, j * TILE : (j + 1) * TILE] = pick
    pl.semaphore_wait(barrier, len(partners))

    def send(src, dst, send_sem, recv_sem, to):
        copy = pltpu.make_async_remote_copy(
            src_ref=src, dst_ref=dst, send_sem=send_sem, recv_sem=recv_sem, device_id=to, device_id_type=MESH
        )
        copy.start()
        return copy

    def finish_all(copies):
        for copy in copies:
            copy.wait()

    own = pt_out.at[z, k]
    near = send(own, own, p_send.at[0], p_recv.at[0], sibling)
    far = {d: send(own, own, p_send.at[d], p_recv.at[d], along_z(d)) for d in (1, 3, 2)}

    def source(d):
        return lax.rem(z + 4 - d, 4)

    def relay(d):
        far[d].wait_recv()
        block = pt_out.at[source(d), k]
        return send(block, block, p_send.at[3 + d], p_recv.at[3 + d], sibling)

    def lanes(d):
        return (along_x, along_y, x, y) if d in (0, 3) else (along_y, along_x, y, x)

    def cross(chunks):
        for d in chunks:
            for j in range(tiles):
                spread = jnp.zeros((2, width, TILE), BF16)
                for i in range(max(j - spare, 0), min(j, active - 1) + 1):
                    spread = jnp.where(tl_ref[i] == j, pt_out[source(d), :, :, i * TILE : (i + 1) * TILE], spread)
                wide[d, :, j * TILE : (j + 1) * TILE] = spread.reshape(pair, TILE)
        lhs = jnp.concatenate([wide[d] for d in chunks], axis=0)
        for t in range(4):
            rhs = t_out[:, :, t * part : (t + 1) * part].reshape(tiles * TILE, part)
            product = dot(lhs, rhs, ((1,), (0,))).astype(BF16)
            for i, d in enumerate(chunks):
                s1[d, t] = product[i * pair : (i + 1) * pair]
        for d in chunks:
            a, _, ma, _ = lanes(d)
            stage1[d] = [
                send(s1.at[d, lax.rem(ma + e, 4)], l1.at[d, e - 1], c_send.at[9 * d + e - 1], c_recv.at[9 * d + e - 1], a(e))
                for e in (2, 1, 3)
            ]

    def second(d):
        _, b, ma, mb = lanes(d)
        finish_all(stage1[d])
        total = s1[d, ma].astype(F32)
        for e in range(3):
            total = total + l1[d, e].astype(F32)
        s2[d, mb] = total.astype(BF16)
        stage2[d] = [
            send(s2.at[d, mb], s2.at[d, mb], c_send.at[9 * d + 2 + e], c_recv.at[9 * d + 2 + e], b(e)) for e in (2, 1, 3)
        ]

    def third(d):
        a, _, ma, _ = lanes(d)
        finish_all(stage2[d])
        total = s2[d, 0].astype(F32)
        for e in range(1, 4):
            total = total + s2[d, e].astype(F32)
        block = cr_out.at[source(d), ma]
        block[...] = total.astype(BF16)
        stage3.extend(send(block, block, c_send.at[9 * d + 5 + e], c_recv.at[9 * d + 5 + e], a(e)) for e in (2, 1, 3))

    stage1, stage2, stage3 = {}, {}, []
    near.wait_recv()
    finish_all(loads)
    cross((0,))
    relays = [relay(1), relay(3)]
    for copy in relays:
        copy.wait_recv()
    cross((1, 3))
    relays.append(relay(2))
    relays[2].wait_recv()

    everything = pt_out[...].reshape(n, active * TILE)
    half = pt_out[pl.ds(2 * k, 2)].reshape(n // 2, active * TILE)
    gx[x] = dot(half, everything, ((1,), (1,))).astype(BF16)
    over_x = [send(gx.at[x], gx.at[x], g_send.at[e - 1], g_recv.at[e - 1], along_x(e)) for e in (2, 1, 3)]
    cross((2,))

    second(0)
    finish_all(over_x)
    gy[y] = (gx[0].astype(F32) + gx[1].astype(F32) + gx[2].astype(F32) + gx[3].astype(F32)).astype(BF16)
    over_y = [send(gy.at[y], gy.at[y], g_send.at[2 + e], g_recv.at[2 + e], along_y(e)) for e in (2, 1, 3)]
    second(1)
    second(3)
    second(2)
    finish_all(over_y)
    gz[k] = gy[0].astype(F32) + gy[1].astype(F32) + gy[2].astype(F32) + gy[3].astype(F32)
    swap = send(gz.at[k], gz.at[k], g_send.at[6], g_recv.at[6], sibling)
    third(0)
    swap.wait()
    aug[:, :n] = gz[...].reshape(n, n)
    eye = lax.broadcasted_iota(jnp.int32, (n, n), 0) == lax.broadcasted_iota(jnp.int32, (n, n), 1)
    aug[:, n:] = jnp.where(eye, 1.0, 0.0)
    steps = factor(aug, u_out, m_out, n, 32)
    for _ in range(4):
        next(steps)
    third(1)
    third(3)
    for _ in range(4):
        next(steps)
    third(2)
    for _ in steps:
        pass
    finish_all(stage3)
    near.wait_send()
    for copy in relays:
        copy.wait_send()
    for copy in far.values():
        copy.wait_send()


def finish(tl_ref, t_ref, pt_ref, cr_ref, u_ref, m_ref, tri_ref, top_hbm, up_hbm, coeff, tops, outs, top_sem, out_sem):
    n = m_ref.shape[0]
    active = tl_ref.shape[0]
    tri_ref[...] = u_ref[...]
    m = m_ref[...]
    mh = m.astype(BF16)
    ml = (m - mh.astype(F32)).astype(BF16)
    copies = []
    for q in range(4):
        part = cr_ref[:, q].reshape(n, 512)
        top = dot(mh, part, ((1,), (0,))) + dot(ml, part, ((1,), (0,)))
        tops[q] = top.T
        copy = pltpu.make_async_copy(tops.at[q], top_hbm.at[pl.ds(q * 512, 512)], top_sem.at[q])
        copy.start()
        copies.append(copy)
        tb = top.astype(BF16)
        coeff[:, q * 512 : (q + 1) * 512] = (dot(mh, tb, ((0,), (0,))) + dot(ml, tb, ((0,), (0,)))).astype(BF16)
    pending = [None] * 3
    for i in range(active // 2):
        slot = i % 3
        if pending[slot] is not None:
            pending[slot].wait()
        cols = pt_ref[:, :, :, i * 256 : (i + 1) * 256].reshape(n, 256)
        product = dot(cols, coeff[...], ((0,), (0,)))
        outs[slot, :128] = (t_ref[tl_ref[2 * i]].astype(F32) - product[:128]).astype(BF16)
        outs[slot, 128:] = (t_ref[tl_ref[2 * i + 1]].astype(F32) - product[128:]).astype(BF16)
        copy = pltpu.make_async_copy(outs.at[slot], up_hbm.at[pl.ds(i * 256, 256)], out_sem.at[slot])
        copy.start()
        pending[slot] = copy
    for copy in pending + copies:
        copy.wait()


def call_finish(tile_list, t, pt, cr, u, m):
    vmem = pl.BlockSpec(memory_space=pltpu.VMEM)
    smem = pl.BlockSpec(memory_space=pltpu.SMEM)
    anywhere = pl.BlockSpec(memory_space=pl.ANY)
    dma = pltpu.SemaphoreType.DMA
    n = m.shape[0]
    cols = t.shape[2]
    active = tile_list.shape[0]
    return pl.pallas_call(
        finish,
        out_shape=(
            jax.ShapeDtypeStruct((n, n), F32),
            jax.ShapeDtypeStruct((cols, n), F32),
            jax.ShapeDtypeStruct((active * TILE, cols), BF16),
        ),
        in_specs=[smem] + [vmem] * 5,
        out_specs=[vmem, anywhere, anywhere],
        scratch_shapes=[
            pltpu.VMEM((n, cols), BF16),
            pltpu.VMEM((4, cols // 4, n), F32),
            pltpu.VMEM((3, 2 * TILE, cols), BF16),
            dma((4,)),
            dma((3,)),
        ],
        compiler_params=pltpu.CompilerParams(vmem_limit_bytes=24 * 2**20),
    )(tile_list, t, pt, cr, u, m)


def local(panel, trailing, tile_list):
    rows, width = panel.shape
    cols = trailing.shape[1]
    active = tile_list.shape[0]
    tiles = rows // TILE
    n = 8 * width
    vmem = pl.BlockSpec(memory_space=pltpu.VMEM)
    smem = pl.BlockSpec(memory_space=pltpu.SMEM)
    hbm = pl.BlockSpec(memory_space=pltpu.HBM)
    dma = pltpu.SemaphoreType.DMA
    t, pt, cr, u, m = pl.pallas_call(
        fetch_and_reduce,
        out_shape=(
            pltpu.VMEM((tiles, TILE, cols), BF16),
            pltpu.VMEM((4, 2, width, active * TILE), BF16),
            pltpu.VMEM((4, 4, 2 * width, cols // 4), BF16),
            pltpu.VMEM((n, n), F32),
            pltpu.VMEM((n, n), F32),
        ),
        in_specs=[smem, vmem, hbm],
        out_specs=[vmem] * 5,
        scratch_shapes=[
            pltpu.VMEM((4, 2 * width, rows), BF16),
            pltpu.VMEM((4, n // 2, n), BF16),
            pltpu.VMEM((4, n // 2, n), BF16),
            pltpu.VMEM((2, n // 2, n), F32),
            pltpu.VMEM((n, 2 * n), F32),
            pltpu.VMEM((4, 4, 2 * width, cols // 4), BF16),
            pltpu.VMEM((4, 3, 2 * width, cols // 4), BF16),
            pltpu.VMEM((4, 4, 2 * width, cols // 4), BF16),
            dma((6,)),
            dma((7,)),
            dma((7,)),
            dma((7,)),
            dma((7,)),
            dma((36,)),
            dma((36,)),
        ],
        compiler_params=pltpu.CompilerParams(collective_id=0, has_side_effects=True, vmem_limit_bytes=24 * 2**20),
    )(tile_list, panel.T, pltpu.with_memory_space_constraint(trailing.reshape(tiles, TILE, cols), pltpu.HBM))
    return call_finish(tile_list, t, pt, cr, u, m)


def solution(mesh):
    return jax.shard_map(
        local,
        mesh=mesh,
        in_specs=(P("row", "col"), P("row", "col"), P("row")),
        out_specs=(P(), P("col", None), P("row", "col")),
        check_vma=False,
    )
```

time: 186 us -> 63.1 us (0.34)
  Pallas kernels: 0 us -> 60.6 us
  other arithmetic: 57.3 us -> 0 us
  waiting for transfers between devices: 45.1 us -> 0 us
  matrix products: 28.8 us -> 0 us
  local copies, waits for them, and re-layouts: 24.5 us -> 1.57 us
  between operations: 15.5 us -> 0.81 us
  starting transfers between devices: 13.6 us -> 0 us
    pallas_call x0 -> x2, Pallas kernels: none -> 60.6 us  [the longest x1 51.1 us: local(): pl.pallas_call(fetch_and_reduce, out_shape=(pltpu.VMEM((tiles, TILE, cols...]
    another operation x9 -> x0, other arithmetic: 54.5 us -> none  [the longest x6 34 us: local(): lower_factor = jnp.linalg.cholesky(gram_matrix)]
    all_to_all x2 -> x0, waiting for transfers between devices: 25.3 us -> none  [sent_to_all(): return lax.all_to_all(copies, axis, split_axis=0, concat_axis=0, tiled=True)]
    psum x1 -> x0, waiting for transfers between devices: 19.7 us -> none  [local(): cross_sum = lax.psum(local_cross, 'row')]
    dot_general x3 -> x0, matrix products: 19.2 us -> none  [the longest x1 9.5 us: local(): lax.dot_general(act_panel, coeff, (((1,), (1,)), ((), ())), preferred_ele...]
    all_to_all x2 -> x0, starting transfers between devices: 13.6 us -> none  [sent_to_all(): return lax.all_to_all(copies, axis, split_axis=0, concat_axis=0, tiled=True)]
    gather x2 -> x0, local copies, waits for them, and re-layouts: 11.1 us -> none  [pick_tiles(): return jnp.take(tiled, tile_list, axis=0).reshape(-1, whole.shape[1])]
    another operation x8 -> x0, matrix products: 9.63 us -> none  [the longest x3 4.69 us: local(): jax.scipy.linalg.solve_triangular(lower_factor, top_rows.T, lower=True, t...]
  transfers between devices with their start and end apart: 3 -> 0, of which waited for: 3 -> 0; matrix products, arithmetic and copies ran while one was open for 45% -> 0% of each run, Pallas kernels for 0% -> 0%
where the time goes in v2:
time: 63.1 us; the launch traced here: 62.9 us
  Pallas kernels  60.6 us (96%)
  local copies, waits for them, and re-layouts  1.57 us (2%)
  between operations  0.81 us (1%)
    pallas_call x1, Pallas kernels, local(): pl.pallas_call(fetch_and_reduce, out_shape=(pltpu.VMEM((tiles, TILE, cols...  51.1 us
    pallas_call x1, Pallas kernels, call_finish(): pl.pallas_call(finish, out_shape=(jax.ShapeDtypeStruct((n, n), F32), jax....  9.48 us
    unnamed x4, local copies, waits for them, and re-layouts  1.57 us

profile of v2, /device:TPU:1, one launch (start us, length us, event | category | flops | bytes accessed | tf_op | source)
XLA Modules:
  0.0 62.9 jit_solution(12081301299326559913)
XLA Ops:
  0.6 0.0 copy-start
  0.6 0.9 %copy-done = bf16[3072,32]{0,1:T(8,128)(2,1)S(1)} copy-done((bf16[3072,32]{0,1:T(8,128)(2,1)S(1)}, bf16[3072,32]{0,1:T(8,128)(2,1)}, u32[]{:S(2)}) %copy-start) | copy-done | bytes 196632
  1.6 0.0 copy-start.1
  1.6 0.7 %copy-done.1 = s32[22]{0:T(128)S(1)} copy-done((s32[22]{0:T(128)S(1)}, s32[22]{0:T(128)}, u32[]{:S(2)}) %copy-start.1) | copy-done | bytes 112
  2.2 51.1 %shard_map.58 = (bf16[24,128,2048]{2,1,0:T(8,128)(2,1)S(1)}, bf16[4,2,32,2816]{3,2,1,0:T(8,128)(2,1)S(1)}, bf16[4,4,64,512]{3,2,1,0:T(8,128)(2,1)S(1)}, f32[256,256]{1,0:T(8,128)S(1)}, f32[256,256]{1,0:T(8,128)S(1)}) custom-call(s32[22]{0:T(128)S(1)} %copy-done.1, bf16[32,3072]{1,0:T(8,128)(2,1)S(1)} %bitcast.2, bf16[24,128,2048]{2,1,0:T(8,128)(2,1)} %bitcast.3), custom_call_target="tpu_custom_call" | custom-call | tf_op jit(solution)/shard_map/pallas_call | solution.py:309
  53.3 9.5 %shard_map.59 = (f32[256,256]{1,0:T(8,128)}, f32[2048,256]{1,0:T(8,128)}, bf16[2816,2048]{1,0:T(8,128)(2,1)}) custom-call(s32[22]{0:T(128)S(1)} %copy-done.1, bf16[24,128,2048]{2,1,0:T(8,128)(2,1)S(1)} %get-tuple-element.8.t_ref, bf16[4,2,32,2816]{3,2,1,0:T(8,128)(2,1)S(1)} %get-tuple-element.9.pt_ref, bf16[4,4,64,512]{3,2,1,0:T(8,128)(2,1)S(1)} %get-tuple-element.10.cr_ref, ...), custom_call_target="tpu_custom_call" | custom-call | tf_op jit(solution)/shard_map/pallas_call | solution.py:279
Async XLA Ops:
  0.6 0.9 %copy-start = (bf16[3072,32]{0,1:T(8,128)(2,1)S(1)}, bf16[3072,32]{0,1:T(8,128)(2,1)}, u32[]{:S(2)}) copy-start(bf16[3072,32]{0,1:T(8,128)(2,1)} %param.3) | copy-start | bytes 589828
  1.6 0.7 %copy-start.1 = (s32[22]{0:T(128)S(1)}, s32[22]{0:T(128)}, u32[]{:S(2)}) copy-start(s32[22]{0:T(128)} %tl_ref.3) | copy-start | bytes 268

commit v3 on v2

--- a/solution.py
+++ b/solution.py
@@ -75,9 +75,9 @@
 
 
 def fetch_and_reduce(
-    tl_ref, pt_ref, t_hbm,
-    t_out, pt_out, cr_out, u_out, m_out,
-    wide, gx, gy, gz, aug, s1, l1, s2,
+    tl_hbm, pt_hbm, t_hbm,
+    t_out, p_out, cr_out, u_out, m_out,
+    tl_ref, pt_ref, pt_out, wide, gx, gy, gz, aug, s1, l1, s2,
     t_sem, p_send, p_recv, g_send, g_recv, c_send, c_recv,
 ):
     width, active = pt_ref.shape[0], tl_ref.shape[0]
@@ -85,7 +85,7 @@
     pair = 2 * width
     tiles = t_out.shape[0]
     spare = tiles - active
-    part = t_out.shape[2] // 4
+    part = t_out.shape[2] // 8
     r, c = lax.axis_index("row"), lax.axis_index("col")
     x, y, z, k = r // 4, lax.rem(r, 4), c // 2, lax.rem(c, 2)
 
@@ -105,12 +105,17 @@
     for partner in partners:
         pl.semaphore_signal(barrier, inc=1, device_id=partner, device_id_type=MESH)
 
+    early = [pltpu.make_async_copy(tl_hbm, tl_ref, t_sem.at[6]), pltpu.make_async_copy(pt_hbm, pt_ref, t_sem.at[7])]
+    for copy in early:
+        copy.start()
     loads = []
     for i in range(6):
         copy = pltpu.make_async_copy(t_hbm.at[pl.ds(4 * i, 4)], t_out.at[pl.ds(4 * i, 4)], t_sem.at[i])
         copy.start()
         loads.append(copy)
 
+    for copy in early:
+        copy.wait()
     for j in range(active):
         pick = pt_ref[:, (j + spare) * TILE : (j + spare + 1) * TILE]
         for i in reversed(range(spare)):
@@ -141,8 +146,8 @@
         block = pt_out.at[source(d), k]
         return send(block, block, p_send.at[3 + d], p_recv.at[3 + d], sibling)
 
-    def lanes(d):
-        return (along_x, along_y, x, y) if d in (0, 3) else (along_y, along_x, y, x)
+    def lanes(h):
+        return (along_x, along_y, x, y) if h == 0 else (along_y, along_x, y, x)
 
     def cross(chunks):
         for d in chunks:
@@ -152,38 +157,45 @@
                     spread = jnp.where(tl_ref[i] == j, pt_out[source(d), :, :, i * TILE : (i + 1) * TILE], spread)
                 wide[d, :, j * TILE : (j + 1) * TILE] = spread.reshape(pair, TILE)
         lhs = jnp.concatenate([wide[d] for d in chunks], axis=0)
-        for t in range(4):
-            rhs = t_out[:, :, t * part : (t + 1) * part].reshape(tiles * TILE, part)
-            product = dot(lhs, rhs, ((1,), (0,))).astype(BF16)
-            for i, d in enumerate(chunks):
-                s1[d, t] = product[i * pair : (i + 1) * pair]
-        for d in chunks:
-            a, _, ma, _ = lanes(d)
-            stage1[d] = [
-                send(s1.at[d, lax.rem(ma + e, 4)], l1.at[d, e - 1], c_send.at[9 * d + e - 1], c_recv.at[9 * d + e - 1], a(e))
-                for e in (2, 1, 3)
-            ]
+        for h in range(2):
+            for t in range(2):
+                at = (2 * h + t) * 2 * part
+                rhs = t_out[:, :, at : at + 2 * part].reshape(tiles * TILE, 2 * part)
+                product = dot(lhs, rhs, ((1,), (0,))).astype(BF16)
+                for i, d in enumerate(chunks):
+                    s1[d, h, 2 * t] = product[i * pair : (i + 1) * pair, :part]
+                    s1[d, h, 2 * t + 1] = product[i * pair : (i + 1) * pair, part:]
+            a, _, ma, _ = lanes(h)
+            for d in chunks:
+                sem = 9 * (2 * d + h) - 1
+                stage1[d, h] = [
+                    send(s1.at[d, h, lax.rem(ma + e, 4)], l1.at[d, h, e - 1], c_send.at[sem + e], c_recv.at[sem + e], a(e))
+                    for e in (2, 1, 3)
+                ]
 
     def second(d):
-        _, b, ma, mb = lanes(d)
-        finish_all(stage1[d])
-        total = s1[d, ma].astype(F32)
-        for e in range(3):
-            total = total + l1[d, e].astype(F32)
-        s2[d, mb] = total.astype(BF16)
-        stage2[d] = [
-            send(s2.at[d, mb], s2.at[d, mb], c_send.at[9 * d + 2 + e], c_recv.at[9 * d + 2 + e], b(e)) for e in (2, 1, 3)
-        ]
+        for h in range(2):
+            _, b, ma, mb = lanes(h)
+            finish_all(stage1[d, h])
+            total = s1[d, h, ma].astype(F32)
+            for e in range(3):
+                total = total + l1[d, h, e].astype(F32)
+            block = s2.at[d, h, mb]
+            block[...] = total.astype(BF16)
+            sem = 9 * (2 * d + h) + 2
+            stage2[d, h] = [send(block, block, c_send.at[sem + e], c_recv.at[sem + e], b(e)) for e in (2, 1, 3)]
 
     def third(d):
-        a, _, ma, _ = lanes(d)
-        finish_all(stage2[d])
-        total = s2[d, 0].astype(F32)
-        for e in range(1, 4):
-            total = total + s2[d, e].astype(F32)
-        block = cr_out.at[source(d), ma]
-        block[...] = total.astype(BF16)
-        stage3.extend(send(block, block, c_send.at[9 * d + 5 + e], c_recv.at[9 * d + 5 + e], a(e)) for e in (2, 1, 3))
+        for h in range(2):
+            a, _, ma, _ = lanes(h)
+            finish_all(stage2[d, h])
+            total = s2[d, h, 0].astype(F32)
+            for e in range(1, 4):
+                total = total + s2[d, h, e].astype(F32)
+            block = cr_out.at[source(d), h, ma]
+            block[...] = total.astype(BF16)
+            sem = 9 * (2 * d + h) + 5
+            stage3.extend(send(block, block, c_send.at[sem + e], c_recv.at[sem + e], a(e)) for e in (2, 1, 3))
 
     stage1, stage2, stage3 = {}, {}, []
     near.wait_recv()
@@ -193,6 +205,7 @@
     for copy in relays:
         copy.wait_recv()
     cross((1, 3))
+    second(0)
     relays.append(relay(2))
     relays[2].wait_recv()
 
@@ -202,26 +215,25 @@
     over_x = [send(gx.at[x], gx.at[x], g_send.at[e - 1], g_recv.at[e - 1], along_x(e)) for e in (2, 1, 3)]
     cross((2,))
 
-    second(0)
+    for i in range(0, active * TILE, 2 * TILE):
+        p_out[i : i + 2 * TILE, :] = pt_out[:, :, :, i : i + 2 * TILE].reshape(n, 2 * TILE).T
+    second(1)
+    second(3)
     finish_all(over_x)
     gy[y] = (gx[0].astype(F32) + gx[1].astype(F32) + gx[2].astype(F32) + gx[3].astype(F32)).astype(BF16)
     over_y = [send(gy.at[y], gy.at[y], g_send.at[2 + e], g_recv.at[2 + e], along_y(e)) for e in (2, 1, 3)]
-    second(1)
-    second(3)
     second(2)
+    third(0)
     finish_all(over_y)
     gz[k] = gy[0].astype(F32) + gy[1].astype(F32) + gy[2].astype(F32) + gy[3].astype(F32)
     swap = send(gz.at[k], gz.at[k], g_send.at[6], g_recv.at[6], sibling)
-    third(0)
+    third(1)
+    third(3)
     swap.wait()
     aug[:, :n] = gz[...].reshape(n, n)
     eye = lax.broadcasted_iota(jnp.int32, (n, n), 0) == lax.broadcasted_iota(jnp.int32, (n, n), 1)
     aug[:, n:] = jnp.where(eye, 1.0, 0.0)
     steps = factor(aug, u_out, m_out, n, 32)
-    for _ in range(4):
-        next(steps)
-    third(1)
-    third(3)
     for _ in range(4):
         next(steps)
     third(2)
@@ -235,44 +247,41 @@
         copy.wait_send()
 
 
-def finish(tl_ref, t_ref, pt_ref, cr_ref, u_ref, m_ref, tri_ref, top_hbm, up_hbm, coeff, tops, outs, top_sem, out_sem):
+def finish(tl_ref, t_ref, p_ref, cr_ref, u_ref, m_ref, tri_ref, top_hbm, up_hbm, tops, outs, top_sem, out_sem):
     n = m_ref.shape[0]
     active = tl_ref.shape[0]
+    part = t_ref.shape[2] // 4
     tri_ref[...] = u_ref[...]
     m = m_ref[...]
     mh = m.astype(BF16)
     ml = (m - mh.astype(F32)).astype(BF16)
     copies = []
     for q in range(4):
-        part = cr_ref[:, q].reshape(n, 512)
-        top = dot(mh, part, ((1,), (0,))) + dot(ml, part, ((1,), (0,)))
+        cols = slice(q * part, (q + 1) * part)
+        blocks = [cr_ref[:, q // 2, 2 * (q % 2) + e].reshape(n, part // 2) for e in range(2)]
+        cross = jnp.concatenate(blocks, axis=1)
+        top = dot(mh, cross, ((1,), (0,))) + dot(ml, cross, ((1,), (0,)))
+        coeff = dot(mh, top.astype(BF16), ((0,), (0,))).astype(BF16)
         tops[q] = top.T
-        copy = pltpu.make_async_copy(tops.at[q], top_hbm.at[pl.ds(q * 512, 512)], top_sem.at[q])
+        copy = pltpu.make_async_copy(tops.at[q], top_hbm.at[pl.ds(q * part, part)], top_sem.at[q])
         copy.start()
         copies.append(copy)
-        tb = top.astype(BF16)
-        coeff[:, q * 512 : (q + 1) * 512] = (dot(mh, tb, ((0,), (0,))) + dot(ml, tb, ((0,), (0,)))).astype(BF16)
-    pending = [None] * 3
-    for i in range(active // 2):
-        slot = i % 3
-        if pending[slot] is not None:
-            pending[slot].wait()
-        cols = pt_ref[:, :, :, i * 256 : (i + 1) * 256].reshape(n, 256)
-        product = dot(cols, coeff[...], ((0,), (0,)))
-        outs[slot, :128] = (t_ref[tl_ref[2 * i]].astype(F32) - product[:128]).astype(BF16)
-        outs[slot, 128:] = (t_ref[tl_ref[2 * i + 1]].astype(F32) - product[128:]).astype(BF16)
-        copy = pltpu.make_async_copy(outs.at[slot], up_hbm.at[pl.ds(i * 256, 256)], out_sem.at[slot])
-        copy.start()
-        pending[slot] = copy
-    for copy in pending + copies:
+        for i in range(active // 2):
+            rows = slice(2 * i * TILE, 2 * (i + 1) * TILE)
+            product = dot(p_ref[rows, :], coeff, ((1,), (0,)))
+            old = jnp.concatenate([t_ref[tl_ref[2 * i + e], :, cols] for e in range(2)], axis=0)
+            outs[rows, cols] = (old.astype(F32) - product).astype(BF16)
+            copy = pltpu.make_async_copy(outs.at[rows, cols], up_hbm.at[rows, cols], out_sem.at[q, i])
+            copy.start()
+            copies.append(copy)
+    for copy in copies:
         copy.wait()
 
 
-def call_finish(tile_list, t, pt, cr, u, m):
+def call_finish(tile_list, t, p, cr, u, m):
     vmem = pl.BlockSpec(memory_space=pltpu.VMEM)
     smem = pl.BlockSpec(memory_space=pltpu.SMEM)
     anywhere = pl.BlockSpec(memory_space=pl.ANY)
-    dma = pltpu.SemaphoreType.DMA
     n = m.shape[0]
     cols = t.shape[2]
     active = tile_list.shape[0]
@@ -286,14 +295,13 @@
         in_specs=[smem] + [vmem] * 5,
         out_specs=[vmem, anywhere, anywhere],
         scratch_shapes=[
-            pltpu.VMEM((n, cols), BF16),
             pltpu.VMEM((4, cols // 4, n), F32),
-            pltpu.VMEM((3, 2 * TILE, cols), BF16),
-            dma((4,)),
-            dma((3,)),
+            pltpu.VMEM((active * TILE, cols), BF16),
+            pltpu.SemaphoreType.DMA((4,)),
+            pltpu.SemaphoreType.DMA((4, active // 2)),
         ],
         compiler_params=pltpu.CompilerParams(vmem_limit_bytes=24 * 2**20),
-    )(tile_list, t, pt, cr, u, m)
+    )(tile_list, t, p, cr, u, m)
 
 
 def local(panel, trailing, tile_list):
@@ -303,40 +311,47 @@
     tiles = rows // TILE
     n = 8 * width
     vmem = pl.BlockSpec(memory_space=pltpu.VMEM)
-    smem = pl.BlockSpec(memory_space=pltpu.SMEM)
     hbm = pl.BlockSpec(memory_space=pltpu.HBM)
     dma = pltpu.SemaphoreType.DMA
-    t, pt, cr, u, m = pl.pallas_call(
+    t, p, cr, u, m = pl.pallas_call(
         fetch_and_reduce,
         out_shape=(
             pltpu.VMEM((tiles, TILE, cols), BF16),
-            pltpu.VMEM((4, 2, width, active * TILE), BF16),
-            pltpu.VMEM((4, 4, 2 * width, cols // 4), BF16),
+            pltpu.VMEM((active * TILE, n), BF16),
+            pltpu.VMEM((4, 2, 4, 2 * width, cols // 8), BF16),
             pltpu.VMEM((n, n), F32),
             pltpu.VMEM((n, n), F32),
         ),
-        in_specs=[smem, vmem, hbm],
+        in_specs=[hbm] * 3,
         out_specs=[vmem] * 5,
         scratch_shapes=[
+            pltpu.SMEM((active,), jnp.int32),
+            pltpu.VMEM((width, rows), BF16),
+            pltpu.VMEM((4, 2, width, active * TILE), BF16),
             pltpu.VMEM((4, 2 * width, rows), BF16),
             pltpu.VMEM((4, n // 2, n), BF16),
             pltpu.VMEM((4, n // 2, n), BF16),
             pltpu.VMEM((2, n // 2, n), F32),
             pltpu.VMEM((n, 2 * n), F32),
-            pltpu.VMEM((4, 4, 2 * width, cols // 4), BF16),
-            pltpu.VMEM((4, 3, 2 * width, cols // 4), BF16),
-            pltpu.VMEM((4, 4, 2 * width, cols // 4), BF16),
-            dma((6,)),
+            pltpu.VMEM((4, 2, 4, 2 * width, cols // 8), BF16),
+            pltpu.VMEM((4, 2, 3, 2 * width, cols // 8), BF16),
+            pltpu.VMEM((4, 2, 4, 2 * width, cols // 8), BF16),
+            dma((8,)),
             dma((7,)),
             dma((7,)),
             dma((7,)),
             dma((7,)),
-            dma((36,)),
-            dma((36,)),
+            dma((72,)),
+            dma((72,)),
         ],
         compiler_params=pltpu.CompilerParams(collective_id=0, has_side_effects=True, vmem_limit_bytes=24 * 2**20),
-    )(tile_list, panel.T, pltpu.with_memory_space_constraint(trailing.reshape(tiles, TILE, cols), pltpu.HBM))
-    return call_finish(tile_list, t, pt, cr, u, m)
+    )(
+        *(
+            pltpu.with_memory_space_constraint(a, pltpu.HBM)
+            for a in (tile_list, panel.T, trailing.reshape(tiles, TILE, cols))
+        )
+    )
+    return call_finish(tile_list, t, p, cr, u, m)
 
 
 def solution(mesh):

time: 63.1 us -> 60.2 us (0.954)
  local copies, waits for them, and re-layouts: 1.57 us -> 0.01 us
  Pallas kernels: 60.6 us -> 59.3 us
    unnamed x4 -> x2, local copies, waits for them, and re-layouts: 1.57 us -> 0.01 us
    pallas_call x1, Pallas kernels: 9.48 us -> 8.28 us  [call_finish(): pl.pallas_call(finish, out_shape=(jax.ShapeDtypeStruct((n, n), F32), jax....]
where the time goes in v3:
time: 60.2 us; the launch traced here: 60.1 us
  Pallas kernels  59.3 us (99%)
  between operations  0.81 us (1%)
    pallas_call x1, Pallas kernels, local(): pl.pallas_call(fetch_and_reduce, out_shape=(pltpu.VMEM((tiles, TILE, cols...  51 us
    pallas_call x1, Pallas kernels, call_finish(): pl.pallas_call(finish, out_shape=(jax.ShapeDtypeStruct((n, n), F32), jax....  8.28 us

profile of v3, /device:TPU:1, one launch (start us, length us, event | category | flops | bytes accessed | tf_op | source)
XLA Modules:
  0.0 60.1 jit_solution(1322787010679696368)
XLA Ops:
  0.6 0.0 copy-start
  0.6 51.0 %shard_map.58 = (bf16[24,128,2048]{2,1,0:T(8,128)(2,1)S(1)}, bf16[2816,256]{1,0:T(8,128)(2,1)S(1)}, bf16[4,2,4,64,256]{4,3,2,1,0:T(8,128)(2,1)S(1)}, f32[256,256]{1,0:T(8,128)S(1)}, f32[256,256]{1,0:T(8,128)S(1)}) custom-call(s32[22]{0:T(128)} %tl_ref.1, bf16[32,3072]{1,0:T(8,128)(2,1)} %bitcast.3, bf16[24,128,2048]{2,1,0:T(8,128)(2,1)} %bitcast.2), custom_call_target="tpu_custom_call" | custom-call | tf_op jit(solution)/shard_map/pallas_call | solution.py:316
  51.7 0.0 copy-done
  51.7 8.3 %shard_map.59 = (f32[256,256]{1,0:T(8,128)}, f32[2048,256]{1,0:T(8,128)}, bf16[2816,2048]{1,0:T(8,128)(2,1)}) custom-call(s32[22]{0:T(128)S(1)} %copy-done, bf16[24,128,2048]{2,1,0:T(8,128)(2,1)S(1)} %get-tuple-element.8.t_ref, bf16[2816,256]{1,0:T(8,128)(2,1)S(1)} %get-tuple-element.9.p_ref, bf16[4,2,4,64,256]{4,3,2,1,0:T(8,128)(2,1)S(1)} %get-tuple-element.10.cr_ref, ...), custom_call_target="tpu_custom_call" | custom-call | tf_op jit(solution)/shard_map/pallas_call | solution.py:288
Async XLA Ops:
  0.6 51.1 %copy-start = (s32[22]{0:T(128)S(1)}, s32[22]{0:T(128)}, u32[]{:S(2)}) copy-start(s32[22]{0:T(128)} %tl_ref.1) | copy-start | bytes 268

commit v4 on v3

--- a/solution.py
+++ b/solution.py
@@ -38,40 +38,47 @@
 
 
 def factor(a_ref, u_ref, m_ref, n, block, p=8):
-    wide = 2 * n // 128
-    rows = lax.broadcasted_iota(jnp.int32, (8, 128), 0)
-
-    def across(column):
-        return jnp.concatenate([column] * wide, axis=1)
+    lane = 128
+    count = 2 * n // lane
+    rows = lax.broadcasted_iota(jnp.int32, (8, lane), 0)
 
     for lo in range(0, n, block):
-        groups = [a_ref[lo + i : lo + i + p, :] for i in range(0, block, p)]
+        groups = [[a_ref[lo + i : lo + i + p, w * lane : (w + 1) * lane] for w in range(count)] for i in range(0, block, p)]
         done = []
         for g in range(block // p):
             at = lo + g * p
-            inv = spread_entries(groups[g][:, at : at + p], p)
-            u = None
+            own, off = at // lane, at % lane
+            live = [w for w in range(count) if (w >= own if w < count // 2 else w - count // 2 <= own)]
+            inv = spread_entries(groups[g][own][:, off : off + p], p)
+            columns = []
             for j in range(p):
-                column = jnp.zeros((8, 128), F32)
+                column = jnp.zeros((8, lane), F32)
                 for i in range(j, p):
                     column = jnp.where(rows == i, inv[i, j], column)
-                term = across(column) * groups[g][j : j + 1, :]
-                u = term if u is None else u + term
-            done.append(u)
+                columns.append(column)
+            u = [jnp.zeros((p, lane), F32)] * count
+            for w in live:
+                u[w] = sum(columns[j] * groups[g][w][j : j + 1, :] for j in range(p))
+            done.append(jnp.concatenate(u, axis=1))
             for h in range(g + 1, block // p):
-                left = [jnp.broadcast_to(groups[h][:, at + q : at + q + 1], (8, 128)) for q in range(p)]
-                rest = groups[h]
-                for j in range(p):
-                    column = sum(left[q] * inv[j, q] for q in range(j + 1))
-                    rest = rest - across(column) * u[j : j + 1, :]
-                groups[h] = rest
+                left = [jnp.broadcast_to(groups[h][own][:, off + q : off + q + 1], (8, lane)) for q in range(p)]
+                lower = [sum(left[q] * inv[j, q] for q in range(j + 1)) for j in range(p)]
+                for w in live:
+                    rest = groups[h][w]
+                    for j in range(p):
+                        rest = rest - lower[j] * u[w][j : j + 1, :]
+                    groups[h][w] = rest
             yield
         full = jnp.concatenate(done, axis=0)
         keep = lax.broadcasted_iota(jnp.int32, (block, n), 1) >= lax.broadcasted_iota(jnp.int32, (block, n), 0) + lo
         u_ref[lo : lo + block, :] = jnp.where(keep, full[:, :n], 0.0)
         m_ref[lo : lo + block, :] = full[:, n:]
-        if lo + block < n:
-            a_ref[lo + block :, :] -= dot(full[:, lo + block : n], full, ((0,), (0,)), HIGH)
+        first = lo + block
+        if first < n:
+            cols = slice(first // lane * lane, n + ((first - 1) // lane + 1) * lane)
+            spans = [(first, first + block), (first + block, n)] if first + block < n else [(first, n)]
+            for a, b in spans:
+                a_ref[a:b, cols] -= dot(full[:, a:b], full[:, cols], ((0,), (0,)), HIGH)
 
 
 def fetch_and_reduce(
@@ -217,24 +224,26 @@
 
     for i in range(0, active * TILE, 2 * TILE):
         p_out[i : i + 2 * TILE, :] = pt_out[:, :, :, i : i + 2 * TILE].reshape(n, 2 * TILE).T
-    second(1)
-    second(3)
     finish_all(over_x)
     gy[y] = (gx[0].astype(F32) + gx[1].astype(F32) + gx[2].astype(F32) + gx[3].astype(F32)).astype(BF16)
     over_y = [send(gy.at[y], gy.at[y], g_send.at[2 + e], g_recv.at[2 + e], along_y(e)) for e in (2, 1, 3)]
+    second(1)
+    second(3)
     second(2)
-    third(0)
     finish_all(over_y)
     gz[k] = gy[0].astype(F32) + gy[1].astype(F32) + gy[2].astype(F32) + gy[3].astype(F32)
     swap = send(gz.at[k], gz.at[k], g_send.at[6], g_recv.at[6], sibling)
-    third(1)
-    third(3)
+    third(0)
     swap.wait()
     aug[:, :n] = gz[...].reshape(n, n)
     eye = lax.broadcasted_iota(jnp.int32, (n, n), 0) == lax.broadcasted_iota(jnp.int32, (n, n), 1)
     aug[:, n:] = jnp.where(eye, 1.0, 0.0)
     steps = factor(aug, u_out, m_out, n, 32)
-    for _ in range(4):
+    for _ in range(3):
+        next(steps)
+    third(1)
+    third(3)
+    for _ in range(6):
         next(steps)
     third(2)
     for _ in steps:

time: 60.2 us -> 57.1 us (0.949)
  Pallas kernels: 59.3 us -> 56.1 us
    pallas_call x1, Pallas kernels: 51 us -> 47.8 us  [local(): pl.pallas_call(fetch_and_reduce, out_shape=(pltpu.VMEM((tiles, TILE, cols...]
where the time goes in v4:
time: 57.1 us; the launch traced here: 56.9 us
  Pallas kernels  56.1 us (98%)
  between operations  0.81 us (1%)
    pallas_call x1, Pallas kernels, local(): pl.pallas_call(fetch_and_reduce, out_shape=(pltpu.VMEM((tiles, TILE, cols...  47.8 us
    pallas_call x1, Pallas kernels, call_finish(): pl.pallas_call(finish, out_shape=(jax.ShapeDtypeStruct((n, n), F32), jax....  8.28 us

profile of v4, /device:TPU:1, one launch (start us, length us, event | category | flops | bytes accessed | tf_op | source)
XLA Modules:
  0.0 56.9 jit_solution(5346262118202934496)
XLA Ops:
  0.6 0.0 copy-start
  0.6 47.8 %shard_map.58 = (bf16[24,128,2048]{2,1,0:T(8,128)(2,1)S(1)}, bf16[2816,256]{1,0:T(8,128)(2,1)S(1)}, bf16[4,2,4,64,256]{4,3,2,1,0:T(8,128)(2,1)S(1)}, f32[256,256]{1,0:T(8,128)S(1)}, f32[256,256]{1,0:T(8,128)S(1)}) custom-call(s32[22]{0:T(128)} %tl_ref.1, bf16[32,3072]{1,0:T(8,128)(2,1)} %bitcast.3, bf16[24,128,2048]{2,1,0:T(8,128)(2,1)} %bitcast.2), custom_call_target="tpu_custom_call" | custom-call | tf_op jit(solution)/shard_map/pallas_call | solution.py:325
  48.5 0.0 copy-done
  48.5 8.3 %shard_map.59 = (f32[256,256]{1,0:T(8,128)}, f32[2048,256]{1,0:T(8,128)}, bf16[2816,2048]{1,0:T(8,128)(2,1)}) custom-call(s32[22]{0:T(128)S(1)} %copy-done, bf16[24,128,2048]{2,1,0:T(8,128)(2,1)S(1)} %get-tuple-element.8.t_ref, bf16[2816,256]{1,0:T(8,128)(2,1)S(1)} %get-tuple-element.9.p_ref, bf16[4,2,4,64,256]{4,3,2,1,0:T(8,128)(2,1)S(1)} %get-tuple-element.10.cr_ref, ...), custom_call_target="tpu_custom_call" | custom-call | tf_op jit(solution)/shard_map/pallas_call | solution.py:297
Async XLA Ops:
  0.6 47.9 %copy-start = (s32[22]{0:T(128)S(1)}, s32[22]{0:T(128)}, u32[]{:S(2)}) copy-start(s32[22]{0:T(128)} %tl_ref.1) | copy-start | bytes 268

commit v5 on v4

--- a/solution.py
+++ b/solution.py
@@ -11,7 +11,6 @@
 MESH = pl.DeviceIdType.MESH
 F32 = jnp.float32
 BF16 = jnp.bfloat16
-HIGH = lax.Precision.HIGHEST
 
 
 def dot(a, b, dims, precision=None):
@@ -76,9 +75,13 @@
         first = lo + block
         if first < n:
             cols = slice(first // lane * lane, n + ((first - 1) // lane + 1) * lane)
+            high = full.astype(BF16)
+            rest = (full - high.astype(F32)).astype(BF16)
+            right = jnp.concatenate([high[:, cols], rest[:, cols], high[:, cols]], axis=0)
             spans = [(first, first + block), (first + block, n)] if first + block < n else [(first, n)]
             for a, b in spans:
-                a_ref[a:b, cols] -= dot(full[:, a:b], full[:, cols], ((0,), (0,)), HIGH)
+                left = jnp.concatenate([high[:, a:b], high[:, a:b], rest[:, a:b]], axis=0)
+                a_ref[a:b, cols] -= dot(left, right, ((0,), (0,)))
 
 
 def fetch_and_reduce(
@@ -204,6 +207,8 @@
             sem = 9 * (2 * d + h) + 5
             stage3.extend(send(block, block, c_send.at[sem + e], c_recv.at[sem + e], a(e)) for e in (2, 1, 3))
 
+    eye = lax.broadcasted_iota(jnp.int32, (n, n), 0) == lax.broadcasted_iota(jnp.int32, (n, n), 1)
+    aug[:, n:] = jnp.where(eye, 1.0, 0.0)
     stage1, stage2, stage3 = {}, {}, []
     near.wait_recv()
     finish_all(loads)
@@ -236,8 +241,6 @@
     third(0)
     swap.wait()
     aug[:, :n] = gz[...].reshape(n, n)
-    eye = lax.broadcasted_iota(jnp.int32, (n, n), 0) == lax.broadcasted_iota(jnp.int32, (n, n), 1)
-    aug[:, n:] = jnp.where(eye, 1.0, 0.0)
     steps = factor(aug, u_out, m_out, n, 32)
     for _ in range(3):
         next(steps)

time: 57.1 us -> 56.4 us (0.988)
  Pallas kernels: 56.1 us -> 55.5 us
    pallas_call x1, Pallas kernels: 47.8 us -> 47.2 us  [local(): pl.pallas_call(fetch_and_reduce, out_shape=(pltpu.VMEM((tiles, TILE, cols...]
where the time goes in v5:
time: 56.4 us; the launch traced here: 56.3 us
  Pallas kernels  55.5 us (98%)
  between operations  0.81 us (1%)
    pallas_call x1, Pallas kernels, local(): pl.pallas_call(fetch_and_reduce, out_shape=(pltpu.VMEM((tiles, TILE, cols...  47.2 us
    pallas_call x1, Pallas kernels, call_finish(): pl.pallas_call(finish, out_shape=(jax.ShapeDtypeStruct((n, n), F32), jax....  8.28 us

profile of v5, /device:TPU:1, one launch (start us, length us, event | category | flops | bytes accessed | tf_op | source)
XLA Modules:
  0.0 56.3 jit_solution(14831250182927911566)
XLA Ops:
  0.6 0.0 copy-start
  0.6 47.2 %shard_map.58 = (bf16[24,128,2048]{2,1,0:T(8,128)(2,1)S(1)}, bf16[2816,256]{1,0:T(8,128)(2,1)S(1)}, bf16[4,2,4,64,256]{4,3,2,1,0:T(8,128)(2,1)S(1)}, f32[256,256]{1,0:T(8,128)S(1)}, f32[256,256]{1,0:T(8,128)S(1)}) custom-call(s32[22]{0:T(128)} %tl_ref.1, bf16[32,3072]{1,0:T(8,128)(2,1)} %bitcast.3, bf16[24,128,2048]{2,1,0:T(8,128)(2,1)} %bitcast.2), custom_call_target="tpu_custom_call" | custom-call | tf_op jit(solution)/shard_map/pallas_call | solution.py:328
  47.9 0.0 copy-done
  47.9 8.3 %shard_map.59 = (f32[256,256]{1,0:T(8,128)}, f32[2048,256]{1,0:T(8,128)}, bf16[2816,2048]{1,0:T(8,128)(2,1)}) custom-call(s32[22]{0:T(128)S(1)} %copy-done, bf16[24,128,2048]{2,1,0:T(8,128)(2,1)S(1)} %get-tuple-element.8.t_ref, bf16[2816,256]{1,0:T(8,128)(2,1)S(1)} %get-tuple-element.9.p_ref, bf16[4,2,4,64,256]{4,3,2,1,0:T(8,128)(2,1)S(1)} %get-tuple-element.10.cr_ref, ...), custom_call_target="tpu_custom_call" | custom-call | tf_op jit(solution)/shard_map/pallas_call | solution.py:300
Async XLA Ops:
  0.6 47.2 %copy-start = (s32[22]{0:T(128)S(1)}, s32[22]{0:T(128)}, u32[]{:S(2)}) copy-start(s32[22]{0:T(128)} %tl_ref.1) | copy-start | bytes 268

commit v6 on v5

--- a/solution.py
+++ b/solution.py
@@ -217,8 +217,8 @@
     for copy in relays:
         copy.wait_recv()
     cross((1, 3))
+    relays.append(relay(2))
     second(0)
-    relays.append(relay(2))
     relays[2].wait_recv()
 
     everything = pt_out[...].reshape(n, active * TILE)

time: 56.4 us -> 56.4 us (level)
  no operation moved by 1% of the time
where the time goes in v6:
time: 56.4 us; the launch traced here: 56.3 us
  Pallas kernels  55.5 us (98%)
  between operations  0.81 us (1%)
    pallas_call x1, Pallas kernels, local(): pl.pallas_call(fetch_and_reduce, out_shape=(pltpu.VMEM((tiles, TILE, cols...  47.2 us
    pallas_call x1, Pallas kernels, call_finish(): pl.pallas_call(finish, out_shape=(jax.ShapeDtypeStruct((n, n), F32), jax....  8.28 us

profile of v6, /device:TPU:1, one launch (start us, length us, event | category | flops | bytes accessed | tf_op | source)
XLA Modules:
  0.0 56.3 jit_solution(13943557586762837306)
XLA Ops:
  0.6 0.0 copy-start
  0.6 47.2 %shard_map.58 = (bf16[24,128,2048]{2,1,0:T(8,128)(2,1)S(1)}, bf16[2816,256]{1,0:T(8,128)(2,1)S(1)}, bf16[4,2,4,64,256]{4,3,2,1,0:T(8,128)(2,1)S(1)}, f32[256,256]{1,0:T(8,128)S(1)}, f32[256,256]{1,0:T(8,128)S(1)}) custom-call(s32[22]{0:T(128)} %tl_ref.1, bf16[32,3072]{1,0:T(8,128)(2,1)} %bitcast.3, bf16[24,128,2048]{2,1,0:T(8,128)(2,1)} %bitcast.2), custom_call_target="tpu_custom_call" | custom-call | tf_op jit(solution)/shard_map/pallas_call | solution.py:328
  47.9 0.0 copy-done
  47.9 8.3 %shard_map.59 = (f32[256,256]{1,0:T(8,128)}, f32[2048,256]{1,0:T(8,128)}, bf16[2816,2048]{1,0:T(8,128)(2,1)}) custom-call(s32[22]{0:T(128)S(1)} %copy-done, bf16[24,128,2048]{2,1,0:T(8,128)(2,1)S(1)} %get-tuple-element.8.t_ref, bf16[2816,256]{1,0:T(8,128)(2,1)S(1)} %get-tuple-element.9.p_ref, bf16[4,2,4,64,256]{4,3,2,1,0:T(8,128)(2,1)S(1)} %get-tuple-element.10.cr_ref, ...), custom_call_target="tpu_custom_call" | custom-call | tf_op jit(solution)/shard_map/pallas_call | solution.py:300
Async XLA Ops:
  0.6 47.2 %copy-start = (s32[22]{0:T(128)S(1)}, s32[22]{0:T(128)}, u32[]{:S(2)}) copy-start(s32[22]{0:T(128)} %tl_ref.1) | copy-start | bytes 268
